TPU v7x, 32 devices: a whole 2x2x4 slice. The times are simulated.
32 devices in a mesh: groups: 2 (over y), replica: 4 (over z), tensor: 4 (over x, core).
Axes of the slice: x: 2, y: 2, z: 4, core: 2. Of those that a mesh axis runs over, the one named last changes fastest.
Arguments:
- normed_token_rows: bfloat16 [6144, 8192], P(('groups', 'replica'), 'tensor'), parts along dimension 0, may hold values from -6 to 6
- request_adapter_index: int32 [192, 1], P(('groups', 'replica')), parts along dimension 0, may hold values from 0 to 3; in each aligned block of 24 rows (0 to 23, 24 to 47, ...) at most 12 rows name the same one
- request_span_index: int32 [192], P(('groups', 'replica')), parts along dimension 0, may hold values from 0 to 255
- key_matrix: bfloat16 [8192, 1024], P('tensor'), may hold values from -0.0625 to 0.0625
- adapter_down_factors: bfloat16 [4, 8192, 64], P('replica', 'tensor'), may hold values from -0.0625 to 0.0625
- adapter_up_factors: bfloat16 [4, 64, 1024], P('replica', None, 'tensor'), may hold values from -0.75 to 0.75
Outputs:
- keys_out: bfloat16 [6144, 1024], P(('groups', 'replica'), 'tensor'), parts along dimension 0
There are 2 independent parts, one for each index of `groups`. A program takes and returns all parts, laid end to end along the dimension named above; an argument that names none is the same for every part. Nothing has to cross between parts.
Inputs may be any that keep to these rules, and one draw needn't show every extreme that they name: `request_adapter_index`: among the 24 requests of one replica no adapter is named more than 12 times; in every draw some replica names some adapter exactly 12 times.
All inputs are finite; a program needn't handle non-finite values.
Results may differ from a plain program's by a relative error of at most 0.0055.
Values may be sent and summed in bfloat16 or wider, within the bound.
A program may use at most 128 MiB of HBM per device.

v0:
```python
import jax
import jax.numpy as jnp
from jax import lax
from jax.sharding import PartitionSpec as P

HEAD = 128


theta_base = 500000.0
adapter_scale = 2.0


def rotate(before, position):
    rows = before.shape[0]
    heads = before.reshape(rows, -1, HEAD)
    half = HEAD // 2
    freq = theta_base ** (-(jnp.arange(half).astype(jnp.float32) * 2.0 / HEAD))
    angle = position.astype(jnp.float32)[:, None] * freq[None, :]
    cosine = jnp.cos(angle)[:, None, :]
    sine = jnp.sin(angle)[:, None, :]
    first = heads[..., :half]
    second = heads[..., half:]
    turned = jnp.concatenate(
        [first * cosine - second * sine, second * cosine + first * sine], axis=-1
    )
    return turned.reshape(rows, -1)


def on_device(
    normed_token_rows,
    request_adapter_index,
    request_span_index,
    key_matrix,
    adapter_down_factors,
    adapter_up_factors,
):
    replicas = lax.axis_size("replica")
    row_count, part_width = normed_token_rows.shape
    requests_here = request_adapter_index.shape[0]
    request_rows = row_count // requests_here
    head_columns = adapter_up_factors.shape[2]
    capacity = max(2, 2 * requests_here // replicas)
    base = lax.psum_scatter(
        jnp.einsum("dc,rd->cr", key_matrix, normed_token_rows, preferred_element_type=jnp.float32),
        "tensor",
        scatter_dimension=0,
        tiled=True,
    ).T
    grouped = normed_token_rows.reshape(requests_here, request_rows, part_width)
    owners = request_adapter_index[:, 0]
    same_owner = owners[:, None] == owners[None, :]
    ordinal = jnp.arange(requests_here, dtype=jnp.int32)
    earlier = ordinal[:, None] > ordinal[None, :]
    slot_of = jnp.sum((same_owner & earlier).astype(jnp.int32), axis=1)
    outgoing = jnp.zeros((replicas, capacity, request_rows, part_width), jnp.bfloat16)
    outgoing = outgoing.at[owners, slot_of].set(grouped)
    partial_sum = jnp.einsum(
        "pcrd,dk->pcrk",
        lax.all_to_all(outgoing, "replica", split_axis=0, concat_axis=0, tiled=True),
        adapter_down_factors[0],
        preferred_element_type=jnp.float32,
    )
    reduced_rows = lax.psum(partial_sum, "tensor").astype(jnp.bfloat16)
    expanded_rows = jnp.einsum(
        "mfvd,dg->mfvg", reduced_rows, adapter_up_factors[0], preferred_element_type=jnp.float32
    )
    lowrank_correction = (expanded_rows * adapter_scale).astype(jnp.bfloat16)
    returned = lax.all_to_all(
        lowrank_correction, "replica", split_axis=0, concat_axis=0, tiled=True
    )
    delta = returned[owners, slot_of]
    before = base + delta.reshape(row_count, head_columns).astype(jnp.float32)
    position = (
        request_span_index[:, None] * request_rows
        + jnp.arange(request_rows, dtype=jnp.int32)[None, :]
    ).reshape(row_count)
    return rotate(before, position).astype(jnp.bfloat16)


def solution(mesh):
    in_specs = (
        P(("groups", "replica"), "tensor"),
        P(("groups", "replica"), None),
        P(("groups", "replica")),
        P("tensor", None),
        P("replica", "tensor", None),
        P("replica", None, "tensor"),
    )
    out_specs = P(("groups", "replica"), "tensor")
    return jax.shard_map(
        on_device, mesh=mesh, in_specs=in_specs, out_specs=out_specs, check_vma=False
    )
```

profile of v0, /device:TPU:1, one launch (start us, length us, event | category | flops | bytes accessed | tf_op | source)
XLA Modules:
  0.0 221.9 jit_solution(6215572978360552784)
XLA Ops:
  6.5 0.0 copy-start
  6.5 0.0 copy-start.1
  6.5 1.0 convert_reduce_fusion
  7.5 0.7 fusion.6
  8.2 3.4 %broadcast_in_dim.2 = bf16[4,12,32,2048]{3,2,1,0:T(8,128)(2,1)} broadcast(bf16[]{:T(256)} %constant.8.clone.1), dimensions={} | broadcast | bytes 6291458 | tf_op jit(solution)/shard_map/broadcast_in_dim | solution.py:55
  11.7 0.0 copy-done.1
  11.7 7.6 %scatter_fusion = bf16[4,12,32,2048]{3,2,1,0:T(8,128)(2,1)} fusion(bf16[4,12,32,2048]{3,2,1,0:T(8,128)(2,1)} %broadcast_in_dim.2, s32[24]{0:T(128)S(1)} %get-tuple-element.5, bf16[24,32,2048]{2,1,0:T(8,128)(2,1)S(1)} %bitcast.37), kind=kCustom, calls=%fused_computation.1 | custom fusion | bytes 9437376 | tf_op jit(solution)/shard_map/scatter | solution.py:56
  19.3 5.5 %all-to-all-start = ((bf16[4,12,32,2048]{3,2,1,0:T(8,128)(2,1)}), bf16[4,12,32,2048]{3,2,1,0:T(8,128)(2,1)}, u32[]{:S(2)}, u32[]{:S(2)}) async-start(bf16[4,12,32,2048]{3,2,1,0:T(8,128)(2,1)} %scatter_fusion), calls=%async_computation.1 | async-start | bytes 12582912 | tf_op jit(solution)/shard_map/all_to_all | solution.py:59
  24.8 0.0 reduce-scatter.2.cloned.1.call-start
  24.8 7.4 %fusion.8 = f32[1024,768]{1,0:T(8,128)} fusion(bf16[2048,1024]{1,0:T(8,128)(2,1)} %param.9, bf16[768,2048]{1,0:T(8,128)(2,1)S(1)} %copy-done.1), kind=kOutput, calls=%fused_computation.27 | convolution fusion | flops 3221225472 | bytes 10485760 | tf_op jit(solution)/shard_map/dc,rd->cr/dot_general | solution.py:44
  32.2 0.0 reduce-scatter.2.cloned.1.call-update
  32.2 0.0 copy-start.2
  32.2 0.0 copy-start.3
  32.2 131.1 %all-to-all-done = bf16[4,12,32,2048]{3,2,1,0:T(8,128)(2,1)} async-done(((bf16[4,12,32,2048]{3,2,1,0:T(8,128)(2,1)}), bf16[4,12,32,2048]{3,2,1,0:T(8,128)(2,1)}, u32[]{:S(2)}, u32[]{:S(2)}) %all-to-all-start) | async-done | bytes 6291488 | tf_op jit(solution)/shard_map/all_to_all | solution.py:59
  163.3 0.0 copy-done
  163.3 4.6 %fusion.1 = f32[4,12,32,64]{3,2,1,0:T(8,128)S(1)} fusion(bf16[4,12,32,2048]{3,2,1,0:T(8,128)(2,1)} %all-to-all-done, bf16[1,2048,64]{1,2,0:T(8,128)(2,1)S(1)} %copy-done), kind=kOutput, calls=%fused_computation.11 | convolution fusion | flops 402653184 | bytes 6946816 | tf_op jit(solution)/shard_map/pcrd,dk->pcrk/dot_general | solution.py:57
  167.9 19.5 %all-reduce.1 = bf16[4,12,32,64]{3,2,1,0:T(8,128)(2,1)S(1)} all-reduce(f32[4,12,32,64]{3,2,1,0:T(8,128)S(1)} %fusion.1), channel_id=1, replica_groups=mesh['groups'=2,'replica'=4,'tensor'=4] {'tensor'}, use_global_device_ids=true, to_apply=%region_3.0 | all-reduce | flops 98304 | bytes 589824 | tf_op jit(solution)/shard_map/psum | solution.py:63
  187.4 0.0 copy-done.2
  187.4 1.2 multiply_convert_fusion
  188.6 3.5 %all-to-all-start.1 = ((bf16[4,12,32,256]{3,2,1,0:T(8,128)(2,1)}), bf16[4,12,32,256]{3,2,1,0:T(8,128)(2,1)S(1)}, u32[]{:S(2)}, u32[]{:S(2)}) async-start(bf16[4,12,32,256]{3,2,1,0:T(8,128)(2,1)} %multiply_convert_fusion), calls=%async_computation.2 | async-start | bytes 1572864 | tf_op jit(solution)/shard_map/all_to_all | solution.py:68
  192.1 0.0 copy-done.3
  192.1 0.1 add_convert_fusion.1
  192.2 0.1 convert_element_type.42
  192.3 0.8 multiply_cosine_fusion
  193.1 18.6 %all-to-all-done.1 = bf16[4,12,32,256]{3,2,1,0:T(8,128)(2,1)S(1)} async-done(((bf16[4,12,32,256]{3,2,1,0:T(8,128)(2,1)}), bf16[4,12,32,256]{3,2,1,0:T(8,128)(2,1)S(1)}, u32[]{:S(2)}, u32[]{:S(2)}) %all-to-all-start.1) | async-done | bytes 786464 | tf_op jit(solution)/shard_map/all_to_all | solution.py:68
  211.7 0.7 gather_fusion
  212.4 0.1 bitcast_convert_fusion
  212.4 0.3 copy.11
  212.7 0.0 reduce-scatter.2.cloned.1.call-done
  212.7 1.3 bitcast_add_fusion
  214.0 0.1 subtract_convert_fusion
  214.2 0.9 copy.15
  (3 shorter events, 0.0 us)
Async XLA Ops:
  6.5 156.8 %copy-start = (bf16[1,2048,64]{1,2,0:T(8,128)(2,1)S(1)}, bf16[1,2048,64]{1,2,0:T(8,128)(2,1)}, u32[]{:S(2)}) copy-start(bf16[1,2048,64]{1,2,0:T(8,128)(2,1)} %param.10) | copy-start | bytes 786436
  6.5 5.1 %copy-start.1 = (bf16[768,2048]{1,0:T(8,128)(2,1)S(1)}, bf16[768,2048]{1,0:T(8,128)(2,1)}, u32[]{:S(2)}) copy-start(bf16[768,2048]{1,0:T(8,128)(2,1)} %param.6) | copy-start | bytes 9437188
  19.3 144.0 %all-to-all-start = ((bf16[4,12,32,2048]{3,2,1,0:T(8,128)(2,1)}), bf16[4,12,32,2048]{3,2,1,0:T(8,128)(2,1)}, u32[]{:S(2)}, u32[]{:S(2)}) async-start(bf16[4,12,32,2048]{3,2,1,0:T(8,128)(2,1)} %scatter_fusion), calls=%async_computation.1 | async-start | bytes 12582912 | tf_op jit(solution)/shard_map/all_to_all | solution.py:59
  24.8 187.9 %reduce-scatter.2.cloned.1.call-start = ((), (), s32[]{:S(2)}) async-start(), calls=%async_computation.3 | async-start | bytes 3932160 | tf_op jit(solution)/shard_map/reduce_scatter | solution.py:43
  32.2 155.2 %copy-start.2 = (bf16[1,64,256]{2,1,0:T(8,128)(2,1)S(1)}, bf16[1,64,256]{2,1,0:T(8,128)(2,1)}, u32[]{:S(2)}) copy-start(bf16[1,64,256]{2,1,0:T(8,128)(2,1)} %param.11) | copy-start | bytes 98308
  32.2 159.9 %copy-start.3 = (s32[24]{0:T(128)S(1)}, s32[24]{0:T(128)}, u32[]{:S(2)}) copy-start(s32[24]{0:T(128)} %param.8) | copy-start | bytes 292
  188.6 23.1 %all-to-all-start.1 = ((bf16[4,12,32,256]{3,2,1,0:T(8,128)(2,1)}), bf16[4,12,32,256]{3,2,1,0:T(8,128)(2,1)S(1)}, u32[]{:S(2)}, u32[]{:S(2)}) async-start(bf16[4,12,32,256]{3,2,1,0:T(8,128)(2,1)} %multiply_convert_fusion), calls=%async_computation.2 | async-start | bytes 1572864 | tf_op jit(solution)/shard_map/all_to_all | solution.py:68
Sparse Core Ops, SparseCore 0:
  32.3 40.0 reduce-scatter.1
where the time goes:
time: 224 us; the launch traced here: 222 us
  waiting for transfers between devices  150 us (67%)
  blocking collectives  19.5 us (9%)
  between operations  13.5 us (6%)
  matrix products  13.2 us (6%)
  local copies, waits for them, and re-layouts  13 us (6%)
  starting transfers between devices  8.97 us (4%)
  other arithmetic  4.01 us (2%)
    all_to_all x1, waiting for transfers between devices, on_device(): lax.all_to_all(outgoing, 'replica', split_axis=0, concat_axis=0, tiled=True)  131 us
    psum x1, blocking collectives, on_device(): reduced_rows = lax.psum(partial_sum, 'tensor').astype(jnp.bfloat16)  19.5 us
    all_to_all x1, waiting for transfers between devices, on_device(): lax.all_to_all(lowrank_correction, 'replica', split_axis=0, concat_axis=0...  18.6 us
    scatter x1, local copies, waits for them, and re-layouts, on_device(): outgoing = outgoing.at[owners, slot_of].set(grouped)  7.64 us
    dot_general x1, matrix products, on_device(): jnp.einsum('dc,rd->cr', key_matrix, normed_token_rows, preferred_element_...  7.37 us
    all_to_all x1, starting transfers between devices, on_device(): lax.all_to_all(outgoing, 'replica', split_axis=0, concat_axis=0, tiled=True)  5.48 us
    dot_general x1, matrix products, on_device(): jnp.einsum('pcrd,dk->pcrk', lax.all_to_all(outgoing, 'replica', split_axi...  4.59 us
  transfers between devices with their start and end apart: 3, of which 2 were waited for; matrix products, arithmetic and copies ran while one was open for 7% of the time, Pallas kernels for 0%

commit v1 on v0

v1 whole, which is shorter than its diff:
```python
import functools
import math

import jax
import jax.numpy as jnp
from jax import lax
from jax.experimental import pallas as pl
from jax.experimental.pallas import tpu as pltpu
from jax.sharding import PartitionSpec as P

HEAD = 128
THETA = 500000.0
SCALE = 2.0
MESH = pl.DeviceIdType.MESH


def kernel(
    sizes,
    x_hbm, adapter_ref, span_ref, k_hbm, down_hbm, up_hbm,
    out_ref,
    xbuf, kbuf, downs, ups, mine, osend, orecv, xsend, xrecv,
    zacc, zsend, zrecv, zchip, zx, rowadapter, cosine, sine, angles,
    x_sem, k_sem, own_sem,
    down_ssem, down_rsem, fwd_ssem, fwd_rsem, up_ssem, up_rsem,
    o_ssem, o_rsem, xs_sem, xr_sem, z_ssem, z_rsem, zx_ssem, zx_rsem,
):
    groups, replicas, chips, chunks = sizes
    rows, width = xbuf.shape
    step = rows // chunks
    rank = downs.shape[1]
    part = rank // groups
    cols = ups.shape[2]
    requests = span_ref.shape[0]
    span_rows = rows // requests
    y = lax.axis_index("groups")
    z = lax.axis_index("replica")
    t = lax.axis_index("tensor")
    x, core = t // 2, t % 2
    partner = x * 2 + (1 - core)

    def chip_at(d):
        return lax.rem(x + d, chips)

    order = list(range(1, chips)) + [0]

    loads = {}
    for d in order:
        for j, who in ((0, 1 - core), (1, core)):
            start = pl.multiple_of((chip_at(d) * 2 + who) * cols, cols)
            loads["k", d, j] = pltpu.make_async_copy(
                k_hbm.at[:, pl.ds(start, cols)],
                kbuf.at[d, :, pl.ds(j * cols, cols)],
                k_sem.at[d, j],
            )
    for m in range(chunks):
        loads["x", m] = pltpu.make_async_copy(
            x_hbm.at[pl.ds(m * step, step)], xbuf.at[pl.ds(m * step, step)], x_sem.at[m]
        )
    loads["down"] = pltpu.make_async_copy(down_hbm, downs.at[z], own_sem.at[0])
    loads["up"] = pltpu.make_async_copy(up_hbm, ups.at[z], own_sem.at[1])
    first = order[0]
    loads["k", first, 0].start()
    loads["k", first, 1].start()
    for m in range(chunks):
        loads["x", m].start()
    for d in order[1:]:
        loads["k", d, 0].start()
        loads["k", d, 1].start()
    loads["down"].start()
    loads["up"].start()

    barrier = pltpu.get_barrier_semaphore()
    peers = 0
    for d in range(1, 2 * chips):
        pl.semaphore_signal(barrier, inc=1, device_id={"tensor": lax.rem(t + d, 2 * chips)}, device_id_type=MESH)
        peers += 1
    for d in range(1, replicas):
        pl.semaphore_signal(barrier, inc=1, device_id={"replica": lax.rem(z + d, replicas)}, device_id_type=MESH)
        peers += 1
    for d in range(1, groups):
        pl.semaphore_signal(barrier, inc=1, device_id={"groups": lax.rem(y + d, groups)}, device_id_type=MESH)
        peers += 1
    pl.semaphore_wait(barrier, peers)

    my_part = pl.ds(pl.multiple_of(y * part, part), part)
    for d in range(1, replicas):
        pltpu.make_async_remote_copy(
            src_ref=down_hbm.at[my_part], dst_ref=downs.at[z, my_part],
            send_sem=down_ssem.at[d], recv_sem=down_rsem.at[d],
            device_id={"replica": lax.rem(z + d, replicas)}, device_id_type=MESH,
        ).start()
    for d in range(1, replicas):
        pltpu.make_async_remote_copy(
            src_ref=up_hbm, dst_ref=ups.at[z],
            send_sem=up_ssem.at[d], recv_sem=up_rsem.at[d],
            device_id={"replica": lax.rem(z + d, replicas)}, device_id_type=MESH,
        ).start()

    def down_wait(d):
        return pltpu.make_async_remote_copy(
            src_ref=down_hbm.at[my_part],
            dst_ref=downs.at[lax.rem(z - d + replicas, replicas), my_part],
            send_sem=down_ssem.at[d], recv_sem=down_rsem.at[d],
            device_id={"replica": lax.rem(z + d, replicas)}, device_id_type=MESH,
        )

    def up_wait(d):
        return pltpu.make_async_remote_copy(
            src_ref=up_hbm, dst_ref=ups.at[lax.rem(z - d + replicas, replicas)],
            send_sem=up_ssem.at[d], recv_sem=up_rsem.at[d],
            device_id={"replica": lax.rem(z + d, replicas)}, device_id_type=MESH,
        )

    def forward(d, g):
        source = lax.rem(z - d + replicas, replicas)
        return pltpu.make_async_remote_copy(
            src_ref=downs.at[source, my_part], dst_ref=downs.at[source, my_part],
            send_sem=fwd_ssem.at[d, g], recv_sem=fwd_rsem.at[d, g],
            device_id={"groups": lax.rem(y + g, groups)}, device_id_type=MESH,
        )

    def forward_wait(d, g):
        source = lax.rem(z - d + replicas, replicas)
        theirs = pl.ds(pl.multiple_of(lax.rem(y - g + groups, groups) * part, part), part)
        return pltpu.make_async_remote_copy(
            src_ref=downs.at[source, theirs], dst_ref=downs.at[source, theirs],
            send_sem=fwd_ssem.at[d, g], recv_sem=fwd_rsem.at[d, g],
            device_id={"groups": lax.rem(y + g, groups)}, device_id_type=MESH,
        )

    def to_partner(d, m):
        rs = pl.ds(m * step, step)
        return pltpu.make_async_remote_copy(
            src_ref=osend.at[d, rs], dst_ref=orecv.at[d, rs],
            send_sem=o_ssem.at[d, m], recv_sem=o_rsem.at[d, m],
            device_id={"tensor": partner}, device_id_type=MESH,
        )

    def to_chip(d, m):
        rs = pl.ds(m * step, step)
        return pltpu.make_async_remote_copy(
            src_ref=xsend.at[d, rs], dst_ref=xrecv.at[d, rs],
            send_sem=xs_sem.at[d, m], recv_sem=xr_sem.at[d, m],
            device_id={"tensor": chip_at(d) * 2 + core}, device_id_type=MESH,
        )

    def product(d, m):
        if (d, m) == (order[0], 0):
            loads["k", d, 0].wait()
            loads["k", d, 1].wait()
        elif m == 0:
            loads["k", d, 0].wait()
            loads["k", d, 1].wait()
        if d == order[0]:
            loads["x", m].wait()
        rs = pl.ds(m * step, step)
        both = jnp.dot(xbuf[rs, :], kbuf[d], preferred_element_type=jnp.float32)
        osend[d, rs, :] = both[:, :cols].astype(jnp.bfloat16)
        to_partner(d, m).start()
        mine[d, rs, :] = both[:, cols:]

    def pass_on(d, m):
        rs = pl.ds(m * step, step)
        to_partner(d, m).wait()
        if d != 0:
            total = mine[d, rs, :] + orecv[d, rs, :].astype(jnp.float32)
            xsend[d, rs, :] = total.astype(jnp.bfloat16)
            to_chip(d, m).start()

    todo = [(d, m) for d in order for m in range(chunks)]
    for i, (d, m) in enumerate(todo):
        product(d, m)
        if i >= 1:
            pass_on(*todo[i - 1])

    for q in range(requests):
        rowadapter[pl.ds(q * span_rows, span_rows), :] = jnp.full((span_rows, rank), adapter_ref[q], jnp.int32)
        angles[pl.ds(q, 1), :] = jnp.full((1, HEAD), span_ref[q] * span_rows, jnp.int32).astype(jnp.float32)
    lane = lax.broadcasted_iota(jnp.int32, (1, HEAD), 1)
    half = HEAD // 2
    index = jnp.where(lane >= half, lane - half, lane).astype(jnp.float32)
    freq = jnp.exp(index * (-2.0 / HEAD * math.log(THETA)))
    sign = jnp.where(lane >= half, 1.0, -1.0)
    start_angle = angles[...] * freq
    row_angle = lax.broadcasted_iota(jnp.int32, (span_rows, HEAD), 0).astype(jnp.float32) * freq
    cos_a, sin_a = jnp.cos(start_angle), jnp.sin(start_angle)
    cos_b, sin_b = jnp.cos(row_angle), jnp.sin(row_angle)
    for q in range(requests):
        rs = pl.ds(q * span_rows, span_rows)
        ca, sa = cos_a[q : q + 1, :], sin_a[q : q + 1, :]
        cosine[rs, :] = ca * cos_b - sa * sin_b
        sine[rs, :] = sign * (sa * cos_b + ca * sin_b)

    def shrink(a, initial):
        value = lax.dot_general(
            xbuf[...], downs[a], (((1,), (1,)), ((), ())), preferred_element_type=jnp.float32
        )
        chosen = jnp.where(rowadapter[...] == a, value, 0.0)
        if initial:
            zacc[...] = chosen
        else:
            zacc[...] += chosen

    loads["down"].wait()
    shrink(z, True)
    pass_on(*todo[-1])
    for d in range(1, replicas):
        down_wait(d).wait()
        for g in range(1, groups):
            forward(d, g).start()
    for d in range(1, replicas):
        for g in range(1, groups):
            forward_wait(d, g).wait()
        shrink(lax.rem(z - d + replicas, replicas), False)

    mid = rows // 2
    quarter = rows // 4
    packed = jnp.concatenate([zacc[:mid, :], zacc[mid:, :]], axis=1)
    for h in range(2):
        zsend[h] = packed[h * quarter : (h + 1) * quarter].astype(jnp.bfloat16)
    z_copy = pltpu.make_async_remote_copy(
        src_ref=zsend, dst_ref=zrecv, send_sem=z_ssem, recv_sem=z_rsem,
        device_id={"tensor": partner}, device_id_type=MESH,
    )
    z_copy.start()
    z_copy.wait()
    chip_sum = [
        packed[h * quarter : (h + 1) * quarter] + zrecv[h].astype(jnp.float32) for h in range(2)
    ]
    for h in range(2):
        zchip[h] = chip_sum[h].astype(jnp.bfloat16)

    def z_over(d, c):
        return pltpu.make_async_remote_copy(
            src_ref=zchip.at[core], dst_ref=zx.at[d, core],
            send_sem=zx_ssem.at[d, c], recv_sem=zx_rsem.at[d, core],
            device_id={"tensor": chip_at(d) * 2 + c}, device_id_type=MESH,
        )

    def z_arrival(d, c):
        return pltpu.make_async_remote_copy(
            src_ref=zchip.at[c], dst_ref=zx.at[d, c],
            send_sem=zx_ssem.at[d, c], recv_sem=zx_rsem.at[d, c],
            device_id={"tensor": chip_at(d) * 2 + c}, device_id_type=MESH,
        )

    for d in range(1, chips):
        for c in range(2):
            z_over(d, c).start()
    loads["up"].wait()
    for d in range(1, replicas):
        up_wait(d).wait()
    for d in range(1, chips):
        for c in range(2):
            z_arrival(d, c).wait()
    sums = []
    for h in range(2):
        total = chip_sum[h]
        for d in range(1, chips):
            total = total + zx[d, h].astype(jnp.float32)
        sums.append(total)
    packed = jnp.concatenate(sums, axis=0)
    shrunk = jnp.concatenate([packed[:, :rank], packed[:, rank:]], axis=0)

    together = 4 if replicas % 4 == 0 else 1
    for d in range(1, chips):
        for m in range(chunks):
            to_chip(d, m).wait()
    for m in range(chunks):
        rs = pl.ds(m * step, step)
        reduced = shrunk[m * step : (m + 1) * step]
        names = rowadapter[rs, :]
        expanded = jnp.zeros((step, cols), jnp.float32)
        for a in range(0, replicas, together):
            masked = [jnp.where(names == a + i, reduced, 0.0) for i in range(together)]
            masked = jnp.concatenate(masked, axis=1) if together > 1 else masked[0]
            expanded += jnp.dot(
                masked.astype(jnp.bfloat16),
                ups[a : a + together].reshape(together * rank, cols),
                preferred_element_type=jnp.float32,
            )
        delta = (expanded * SCALE).astype(jnp.bfloat16).astype(jnp.float32)
        base = mine[0, rs, :] + orecv[0, rs, :].astype(jnp.float32)
        for d in range(1, chips):
            base += xrecv[d, rs, :].astype(jnp.float32)
        before = base + delta
        for h in range(cols // HEAD):
            head = before[:, h * HEAD : (h + 1) * HEAD]
            turned = head * cosine[rs, :] + pltpu.roll(head, half, 1) * sine[rs, :]
            out_ref[rs, h * HEAD : (h + 1) * HEAD] = turned.astype(jnp.bfloat16)


def on_device(sizes, rows, adapters, spans, keys, down, up):
    groups, replicas, chips, chunks = sizes
    row_count, width = rows.shape
    rank, cols = up.shape[1], up.shape[2]
    requests = spans.shape[0]
    bf, f32 = jnp.bfloat16, jnp.float32
    vm, dma = pltpu.VMEM, pltpu.SemaphoreType.DMA
    quarter = row_count // 4
    anywhere = pl.BlockSpec(memory_space=pl.ANY)
    smem = pl.BlockSpec(memory_space=pltpu.SMEM)
    return pl.pallas_call(
        functools.partial(kernel, sizes),
        out_shape=jax.ShapeDtypeStruct((row_count, cols), bf),
        in_specs=[anywhere, smem, smem, anywhere, anywhere, anywhere],
        out_specs=pl.BlockSpec(memory_space=pltpu.VMEM),
        scratch_shapes=[
            vm((row_count, width), bf),
            vm((chips, width, 2 * cols), bf),
            vm((replicas, rank, width), bf),
            vm((replicas, rank, cols), bf),
            vm((chips, row_count, cols), f32),
            vm((chips, row_count, cols), bf),
            vm((chips, row_count, cols), bf),
            vm((chips, row_count, cols), bf),
            vm((chips, row_count, cols), bf),
            vm((row_count, rank), f32),
            vm((2, quarter, 2 * rank), bf),
            vm((2, quarter, 2 * rank), bf),
            vm((2, quarter, 2 * rank), bf),
            vm((chips, 2, quarter, 2 * rank), bf),
            vm((row_count, rank), jnp.int32),
            vm((row_count, HEAD), f32),
            vm((row_count, HEAD), f32),
            vm((requests, HEAD), f32),
            dma((chunks,)), dma((chips, 2)), dma((2,)),
            dma((replicas,)), dma((replicas,)),
            dma((replicas, groups)), dma((replicas, groups)),
            dma((replicas,)), dma((replicas,)),
            dma((chips, chunks)), dma((chips, chunks)),
            dma((chips, chunks)), dma((chips, chunks)),
            dma, dma,
            dma((chips, 2)), dma((chips, 2)),
        ],
        compiler_params=pltpu.CompilerParams(
            collective_id=0, has_side_effects=True, vmem_limit_bytes=48 * 1024 * 1024
        ),
        cost_estimate=pl.CostEstimate(
            flops=2 * row_count * width * (2 * chips * cols + replicas * rank),
            bytes_accessed=2 * width * (row_count + 2 * chips * cols),
            transcendentals=0,
        ),
    )(rows, adapters.reshape(requests), spans, keys, down[0].T, up[0])


def solution(mesh):
    in_specs = (
        P(("groups", "replica"), "tensor"),
        P(("groups", "replica"), None),
        P(("groups", "replica")),
        P("tensor", None),
        P("replica", "tensor", None),
        P("replica", None, "tensor"),
    )
    out_specs = P(("groups", "replica"), "tensor")
    sizes = (mesh.shape["groups"], mesh.shape["replica"], mesh.shape["tensor"] // 2, 3)
    return jax.shard_map(
        functools.partial(on_device, sizes), mesh=mesh, in_specs=in_specs, out_specs=out_specs, check_vma=False
    )
```

time: 224 us -> 39.1 us (0.17)
  waiting for transfers between devices: 150 us -> 0 us
  Pallas kernels: 0 us -> 33.1 us
  blocking collectives: 19.5 us -> 0 us
  between operations: 13.5 us -> 0.01 us
  matrix products: 13.2 us -> 0 us
  starting transfers between devices: 8.97 us -> 0 us
  local copies, waits for them, and re-layouts: 13 us -> 5.65 us
  other arithmetic: 4.01 us -> 0 us
    all_to_all x2 -> x0, waiting for transfers between devices: 150 us -> none  [the longest x1 131 us: on_device(): lax.all_to_all(outgoing, 'replica', split_axis=0, concat_axis=0, tiled=True)]
    pallas_call x0 -> x1, Pallas kernels: none -> 33.1 us  [on_device(): pl.pallas_call(functools.partial(kernel, sizes), out_shape=jax.ShapeDtype...]
    psum x1 -> x0, blocking collectives: 19.5 us -> none  [on_device(): reduced_rows = lax.psum(partial_sum, 'tensor').astype(jnp.bfloat16)]
    dot_general x3 -> x0, matrix products: 13.2 us -> none  [the longest x1 7.37 us: on_device(): jnp.einsum('dc,rd->cr', key_matrix, normed_token_rows, preferred_element_...]
    all_to_all x2 -> x0, starting transfers between devices: 8.97 us -> none  [the longest x1 5.48 us: on_device(): lax.all_to_all(outgoing, 'replica', split_axis=0, concat_axis=0, tiled=True)]
    scatter x1 -> x0, local copies, waits for them, and re-layouts: 7.64 us -> none  [on_device(): outgoing = outgoing.at[owners, slot_of].set(grouped)]
    unnamed x8 -> x11, local copies, waits for them, and re-layouts: 0.02 us -> 5.65 us
    broadcast_in_dim x1 -> x0, local copies, waits for them, and re-layouts: 3.45 us -> none  [on_device(): jnp.zeros((replicas, capacity, request_rows, part_width), jnp.bfloat16)]
  transfers between devices with their start and end apart: 3 -> 0, of which waited for: 2 -> 0; matrix products, arithmetic and copies ran while one was open for 7% -> 0% of each run, Pallas kernels for 0% -> 0%
where the time goes in v1:
time: 39.1 us; the launch traced here: 38.8 us
  Pallas kernels  33.1 us (85%)
  local copies, waits for them, and re-layouts  5.65 us (14%)
    pallas_call x1, Pallas kernels, on_device(): pl.pallas_call(functools.partial(kernel, sizes), out_shape=jax.ShapeDtype...  33.1 us
    unnamed x11, local copies, waits for them, and re-layouts  5.65 us

profile of v1, /device:TPU:1, one launch (start us, length us, event | category | flops | bytes accessed | tf_op | source)
XLA Modules:
  0.0 38.8 jit_solution(2021990503917810534)
XLA Ops:
  0.0 0.0 copy-start
  0.0 1.9 %copy-done = bf16[768,2048]{1,0:T(8,128)(2,1)S(1)} copy-done((bf16[768,2048]{1,0:T(8,128)(2,1)S(1)}, bf16[768,2048]{1,0:T(8,128)(2,1)}, u32[]{:S(2)}) %copy-start) | copy-done | bytes 3145752
  1.9 0.0 copy-start.1
  1.9 0.9 %copy-done.1 = bf16[1,2048,64]{1,2,0:T(8,128)(2,1)S(1)} copy-done((bf16[1,2048,64]{1,2,0:T(8,128)(2,1)S(1)}, bf16[1,2048,64]{1,2,0:T(8,128)(2,1)}, u32[]{:S(2)}) %copy-start.1) | copy-done | bytes 262168
  2.8 0.0 copy-start.2
  2.8 0.8 %copy-done.2 = bf16[1,64,256]{2,1,0:T(8,128)(2,1)S(1)} copy-done((bf16[1,64,256]{2,1,0:T(8,128)(2,1)S(1)}, bf16[1,64,256]{2,1,0:T(8,128)(2,1)}, u32[]{:S(2)}) %copy-start.2) | copy-done | bytes 32792
  3.6 0.0 copy-start.3
  3.6 0.7 %copy-done.3 = s32[24,1]{0,1:T(1,128)S(1)} copy-done((s32[24,1]{0,1:T(1,128)S(1)}, s32[24,1]{0,1:T(1,128)}, u32[]{:S(2)}) %copy-start.3) | copy-done | bytes 120
  4.3 0.0 copy-start.4
  4.3 0.7 %copy-done.4 = s32[24]{0:T(128)S(1)} copy-done((s32[24]{0:T(128)S(1)}, s32[24]{0:T(128)}, u32[]{:S(2)}) %copy-start.4) | copy-done | bytes 120
  4.9 33.1 %shard_map.64 = bf16[768,256]{1,0:T(8,128)(2,1)S(1)} custom-call(bf16[768,2048]{1,0:T(8,128)(2,1)S(1)} %copy-done, s32[24]{0:T(128)S(1)} %bitcast.7, s32[24]{0:T(128)S(1)} %copy-done.4, bf16[2048,1024]{1,0:T(8,128)(2,1)} %k_hbm.1, bf16[64,2048]{1,0:T(8,128)(2,1)S(1)} %bitcast.5, bf16[64,256]{1,0:T(8,128)(2,1)S(1)} %bitcast.6), custom_call_target="tpu_custom_call" | custom-call | flops 4026531840 | bytes 7340032 | tf_op jit(solution)/shard_map/pallas_call | solution.py:303
  38.0 0.7 %copy.8 = bf16[768,256]{1,0:T(8,128)(2,1)} copy(bf16[768,256]{1,0:T(8,128)(2,1)S(1)} %shard_map.64) | data formatting | bytes 786432
Async XLA Ops:
  0.0 1.9 %copy-start = (bf16[768,2048]{1,0:T(8,128)(2,1)S(1)}, bf16[768,2048]{1,0:T(8,128)(2,1)}, u32[]{:S(2)}) copy-start(bf16[768,2048]{1,0:T(8,128)(2,1)} %x_hbm.1) | copy-start | bytes 9437188
  1.9 0.9 %copy-start.1 = (bf16[1,2048,64]{1,2,0:T(8,128)(2,1)S(1)}, bf16[1,2048,64]{1,2,0:T(8,128)(2,1)}, u32[]{:S(2)}) copy-start(bf16[1,2048,64]{1,2,0:T(8,128)(2,1)} %param.10) | copy-start | bytes 786436
  2.8 0.8 %copy-start.2 = (bf16[1,64,256]{2,1,0:T(8,128)(2,1)S(1)}, bf16[1,64,256]{2,1,0:T(8,128)(2,1)}, u32[]{:S(2)}) copy-start(bf16[1,64,256]{2,1,0:T(8,128)(2,1)} %param.11) | copy-start | bytes 98308
  3.6 0.7 %copy-start.3 = (s32[24,1]{0,1:T(1,128)S(1)}, s32[24,1]{0,1:T(1,128)}, u32[]{:S(2)}) copy-start(s32[24,1]{0,1:T(1,128)} %param.7) | copy-start | bytes 292
  4.3 0.7 %copy-start.4 = (s32[24]{0:T(128)S(1)}, s32[24]{0:T(128)}, u32[]{:S(2)}) copy-start(s32[24]{0:T(128)} %span_ref.1) | copy-start | bytes 292

commit v2 on v1

v2 whole, which is shorter than its diff:
```python
import functools
import math

import jax
import jax.numpy as jnp
from jax import lax
from jax.experimental import pallas as pl
from jax.experimental.pallas import tpu as pltpu
from jax.sharding import PartitionSpec as P

HEAD = 128
THETA = 500000.0
SCALE = 2.0
TOGETHER = 4
MESH = pl.DeviceIdType.MESH


def kernel(
    sizes,
    x_hbm, adapter_ref, span_ref, k_hbm, down_hbm, up_hbm,
    out_ref,
    xbuf, kbuf, downs, ups, mine, osend, orecv, xsend, xrecv,
    zacc, zsend, zrecv, zchip, zx, rowadapter, cosine, sine, angles,
    x_sem, k_sem, own_sem,
    down_ssem, down_rsem, fwd_ssem, fwd_rsem, up_ssem, up_rsem,
    o_ssem, o_rsem, xs_sem, xr_sem, z_ssem, z_rsem, zx_ssem, zx_rsem,
):
    groups, replicas, chips, chunks, pieces = sizes
    rows, width = xbuf.shape
    step = rows // chunks
    rank = downs.shape[1]
    part = width // groups
    cols = ups.shape[2]
    requests = span_ref.shape[0]
    span_rows = rows // requests
    y = lax.axis_index("groups")
    z = lax.axis_index("replica")
    t = lax.axis_index("tensor")
    x, core = t // 2, t % 2
    partner = x * 2 + (1 - core)

    def chip_at(d):
        return lax.rem(x + d, chips)

    barrier = pltpu.get_barrier_semaphore()
    peers = 0
    for d in range(1, 2 * chips):
        pl.semaphore_signal(barrier, inc=1, device_id={"tensor": lax.rem(t + d, 2 * chips)}, device_id_type=MESH)
        peers += 1
    for d in range(1, replicas):
        pl.semaphore_signal(barrier, inc=1, device_id={"replica": lax.rem(z + d, replicas)}, device_id_type=MESH)
        peers += 1
    for d in range(1, groups):
        pl.semaphore_signal(barrier, inc=1, device_id={"groups": lax.rem(y + d, groups)}, device_id_type=MESH)
        peers += 1

    order = list(range(1, chips)) + [0]

    loads = {}
    for d in order:
        for j, who in ((0, 1 - core), (1, core)):
            start = pl.multiple_of((chip_at(d) * 2 + who) * cols, cols)
            loads["k", d, j] = pltpu.make_async_copy(
                k_hbm.at[:, pl.ds(start, cols)],
                kbuf.at[d, :, pl.ds(j * cols, cols)],
                k_sem.at[d, j],
            )
    for m in range(chunks):
        loads["x", m] = pltpu.make_async_copy(
            x_hbm.at[pl.ds(m * step, step)], xbuf.at[pl.ds(m * step, step)], x_sem.at[m]
        )
    loads["down"] = pltpu.make_async_copy(down_hbm, downs.at[z], own_sem.at[0])
    loads["up"] = pltpu.make_async_copy(up_hbm, ups.at[z], own_sem.at[1])
    first = order[0]
    loads["k", first, 0].start()
    loads["k", first, 1].start()
    for m in range(chunks):
        loads["x", m].start()
    for d in order[1:]:
        loads["k", d, 0].start()
        loads["k", d, 1].start()
    loads["down"].start()
    loads["up"].start()

    block_of = lax.broadcasted_iota(jnp.int32, (span_rows, TOGETHER * rank), 1) // rank
    for q in range(requests):
        rowadapter[pl.ds(q * span_rows, span_rows), :] = jnp.full((span_rows, TOGETHER * rank), adapter_ref[q], jnp.int32) - block_of
        angles[pl.ds(q, 1), :] = jnp.full((1, HEAD), span_ref[q] * span_rows, jnp.int32).astype(jnp.float32)
    lane = lax.broadcasted_iota(jnp.int32, (1, HEAD), 1)
    half = HEAD // 2
    index = jnp.where(lane >= half, lane - half, lane).astype(jnp.float32)
    freq = jnp.exp(index * (-2.0 / HEAD * math.log(THETA)))
    sign = jnp.where(lane >= half, 1.0, -1.0)
    start_angle = angles[...] * freq
    row_angle = lax.broadcasted_iota(jnp.int32, (span_rows, HEAD), 0).astype(jnp.float32) * freq
    cos_a, sin_a = jnp.cos(start_angle), jnp.sin(start_angle)
    cos_b, sin_b = jnp.cos(row_angle), jnp.sin(row_angle)
    for q in range(requests):
        rs = pl.ds(q * span_rows, span_rows)
        ca, sa = cos_a[q : q + 1, :], sin_a[q : q + 1, :]
        cosine[rs, :] = ca * cos_b - sa * sin_b
        sine[rs, :] = sign * (sa * cos_b + ca * sin_b)

    def product(d, m):
        if (d, m) == (order[0], 0):
            loads["k", d, 0].wait()
            loads["k", d, 1].wait()
        elif m == 0:
            loads["k", d, 0].wait()
            loads["k", d, 1].wait()
        if d == order[0]:
            loads["x", m].wait()
        rs = pl.ds(m * step, step)
        both = jnp.dot(xbuf[rs, :], kbuf[d], preferred_element_type=jnp.float32)
        osend[d, rs, :] = both[:, :cols].astype(jnp.bfloat16)
        mine[d, rs, :] = both[:, cols:]

    todo = [(d, m) for d in order for m in range(chunks)]
    pl.semaphore_wait(barrier, peers)

    def piece(g, p):
        at = lax.rem(y + g + groups, groups) * part + p * (part // pieces)
        return pl.ds(pl.multiple_of(at, 128), part // pieces)

    def group_part(g):
        return pl.ds(pl.multiple_of(lax.rem(y + g + groups, groups) * part, 128), part)

    def hop(a, p, way):
        return pltpu.make_async_remote_copy(
            src_ref=downs.at[a, :, piece(0, p)], dst_ref=downs.at[a, :, piece(0, p)],
            send_sem=down_ssem.at[a, p, (way + 1) // 2], recv_sem=down_rsem.at[a, p],
            device_id={"replica": z + way}, device_id_type=MESH,
        )

    def own_hop(p, way):
        return pltpu.make_async_remote_copy(
            src_ref=down_hbm.at[:, piece(0, p)], dst_ref=downs.at[z, :, piece(0, p)],
            send_sem=down_ssem.at[z, p, (way + 1) // 2], recv_sem=down_rsem.at[z, p],
            device_id={"replica": z + way}, device_id_type=MESH,
        )

    def forward(a, g, p, own):
        cut = piece(0 if own else -g, p)
        return pltpu.make_async_remote_copy(
            src_ref=downs.at[a, :, cut], dst_ref=downs.at[a, :, cut],
            send_sem=fwd_ssem.at[a, g, p], recv_sem=fwd_rsem.at[a, g, p],
            device_id={"groups": lax.rem(y + g, groups)}, device_id_type=MESH,
        )

    def relay(a, p, way):
        hop(a, p, way).wait_recv()
        pl.when((z + way >= 0) & (z + way < replicas))(lambda: hop(a, p, way).start())
        for g in range(1, groups):
            forward(a, g, p, True).start()

    def relay_from(k):
        for p in range(pieces):
            pl.when(z >= k)(lambda: relay(z - k, p, 1))
            pl.when(z + k < replicas)(lambda: relay(z + k, p, -1))

    def relay_end(k):
        for p in range(pieces):
            @pl.when((z >= k) & (z + 1 < replicas))
            def _():
                (own_hop(p, 1) if k == 0 else hop(z - k, p, 1)).wait_send()

            @pl.when((z + k < replicas) & (z >= 1))
            def _():
                (own_hop(p, -1) if k == 0 else hop(z + k, p, -1)).wait_send()

    def up_send(j):
        return pltpu.make_async_remote_copy(
            src_ref=up_hbm, dst_ref=ups.at[z],
            send_sem=up_ssem.at[j], recv_sem=up_rsem.at[j],
            device_id={"replica": lax.rem(z + j, replicas)}, device_id_type=MESH,
        )

    def up_arrival(j):
        return pltpu.make_async_remote_copy(
            src_ref=up_hbm, dst_ref=ups.at[lax.rem(z - j + replicas, replicas)],
            send_sem=up_ssem.at[j], recv_sem=up_rsem.at[j],
            device_id={"replica": lax.rem(z + j, replicas)}, device_id_type=MESH,
        )

    for p in range(pieces):
        pl.when(z + 1 < replicas)(lambda: own_hop(p, 1).start())
        pl.when(z >= 1)(lambda: own_hop(p, -1).start())

    def to_partner(d, m):
        rs = pl.ds(m * step, step)
        return pltpu.make_async_remote_copy(
            src_ref=osend.at[d, rs], dst_ref=orecv.at[d, rs],
            send_sem=o_ssem.at[d, m], recv_sem=o_rsem.at[d, m],
            device_id={"tensor": partner}, device_id_type=MESH,
        )

    def to_chip(d, m):
        rs = pl.ds(m * step, step)
        return pltpu.make_async_remote_copy(
            src_ref=xsend.at[d, rs], dst_ref=xrecv.at[d, rs],
            send_sem=xs_sem.at[d, m], recv_sem=xr_sem.at[d, m],
            device_id={"tensor": chip_at(d) * 2 + core}, device_id_type=MESH,
        )

    def pass_on(d, m):
        rs = pl.ds(m * step, step)
        to_partner(d, m).wait()
        if d != 0:
            total = mine[d, rs, :] + orecv[d, rs, :].astype(jnp.float32)
            xsend[d, rs, :] = total.astype(jnp.bfloat16)
            to_chip(d, m).start()

    hops = 1
    for i, (d, m) in enumerate(todo):
        product(d, m)
        to_partner(d, m).start()
        if i >= 1:
            pass_on(*todo[i - 1])
        if i + 1 >= chunks and hops < replicas:
            relay_from(hops)
            hops += 1
    for k in range(hops, replicas):
        relay_from(k)
    for j in range(1, replicas):
        up_send(j).start()
    pass_on(*todo[-1])

    def shrink(cut):
        kept = None
        for a in range(0, replicas, TOGETHER):
            value = lax.dot_general(
                xbuf[:, cut],
                downs[a : a + TOGETHER, :, cut].reshape(TOGETHER * rank, part),
                (((1,), (1,)), ((), ())),
                preferred_element_type=jnp.float32,
            )
            chosen = jnp.where(rowadapter[...] == a, value, 0.0)
            kept = chosen if kept is None else kept + chosen
        pair = kept[:, : 2 * rank] + kept[:, 2 * rank :]
        return pair + pltpu.roll(pair, rank, 1)

    loads["down"].wait()
    zacc[...] = shrink(group_part(0))
    for m in range(chunks):
        rs = pl.ds(m * step, step)
        base = mine[0, rs, :] + orecv[0, rs, :].astype(jnp.float32)
        for d in range(1, chips):
            to_chip(d, m).wait()
            base += xrecv[d, rs, :].astype(jnp.float32)
        mine[0, rs, :] = base
    for g in range(1, groups):
        for j in range(1, replicas):
            for p in range(pieces):
                forward(lax.rem(z + j, replicas), g, p, False).wait_recv()
    for g in range(1, groups):
        zacc[...] += shrink(group_part(-g))

    mid = rows // 2
    quarter = rows // 4
    low = lax.broadcasted_iota(jnp.int32, (mid, 2 * rank), 1) < rank
    packed = jnp.where(low, zacc[:mid, :], zacc[mid:, :])
    for h in range(2):
        zsend[h] = packed[h * quarter : (h + 1) * quarter].astype(jnp.bfloat16)
    z_copy = pltpu.make_async_remote_copy(
        src_ref=zsend, dst_ref=zrecv, send_sem=z_ssem, recv_sem=z_rsem,
        device_id={"tensor": partner}, device_id_type=MESH,
    )
    z_copy.start()
    z_copy.wait()
    chip_sum = [
        packed[h * quarter : (h + 1) * quarter] + zrecv[h].astype(jnp.float32) for h in range(2)
    ]
    for h in range(2):
        zchip[h] = chip_sum[h].astype(jnp.bfloat16)

    def z_over(d, c):
        return pltpu.make_async_remote_copy(
            src_ref=zchip.at[core], dst_ref=zx.at[d, core],
            send_sem=zx_ssem.at[d, c], recv_sem=zx_rsem.at[d, core],
            device_id={"tensor": chip_at(d) * 2 + c}, device_id_type=MESH,
        )

    def z_arrival(d, c):
        return pltpu.make_async_remote_copy(
            src_ref=zchip.at[c], dst_ref=zx.at[d, c],
            send_sem=zx_ssem.at[d, c], recv_sem=zx_rsem.at[d, c],
            device_id={"tensor": chip_at(d) * 2 + c}, device_id_type=MESH,
        )

    for d in range(1, chips):
        for c in range(2):
            z_over(d, c).start()
    loads["up"].wait()
    for j in range(1, replicas):
        up_arrival(j).wait()
    for k in range(replicas):
        relay_end(k)
    for g in range(1, groups):
        for j in range(1, replicas):
            for p in range(pieces):
                forward(lax.rem(z + j, replicas), g, p, True).wait_send()
    for d in range(1, chips):
        for c in range(2):
            z_arrival(d, c).wait()
    sums = []
    for h in range(2):
        total = chip_sum[h]
        for d in range(1, chips):
            total = total + zx[d, h].astype(jnp.float32)
        sums.append(total)
    packed = jnp.concatenate(sums, axis=0)
    swapped = pltpu.roll(packed, rank, 1)
    shrunk = jnp.concatenate([jnp.where(low, packed, swapped), jnp.where(low, swapped, packed)], axis=0)
    shrunk = jnp.concatenate([shrunk] * (TOGETHER // 2), axis=1)

    for m in range(chunks):
        rs = pl.ds(m * step, step)
        reduced = shrunk[m * step : (m + 1) * step]
        names = rowadapter[rs, :]
        expanded = jnp.zeros((step, cols), jnp.float32)
        for a in range(0, replicas, TOGETHER):
            expanded += jnp.dot(
                jnp.where(names == a, reduced, 0.0).astype(jnp.bfloat16),
                ups[a : a + TOGETHER].reshape(TOGETHER * rank, cols),
                preferred_element_type=jnp.float32,
            )
        delta = (expanded * SCALE).astype(jnp.bfloat16).astype(jnp.float32)
        before = mine[0, rs, :] + delta
        for h in range(cols // HEAD):
            head = before[:, h * HEAD : (h + 1) * HEAD]
            turned = head * cosine[rs, :] + pltpu.roll(head, half, 1) * sine[rs, :]
            out_ref[rs, h * HEAD : (h + 1) * HEAD] = turned.astype(jnp.bfloat16)


def on_device(sizes, rows, adapters, spans, keys, down, up):
    groups, replicas, chips, chunks, pieces = sizes
    row_count, width = rows.shape
    rank, cols = up.shape[1], up.shape[2]
    requests = spans.shape[0]
    bf, f32 = jnp.bfloat16, jnp.float32
    vm, dma = pltpu.VMEM, pltpu.SemaphoreType.DMA
    quarter = row_count // 4
    anywhere = pl.BlockSpec(memory_space=pltpu.HBM)
    smem = pl.BlockSpec(memory_space=pltpu.SMEM)
    return pl.pallas_call(
        functools.partial(kernel, sizes),
        out_shape=jax.ShapeDtypeStruct((row_count, cols), bf),
        in_specs=[anywhere, smem, smem, anywhere, anywhere, anywhere],
        out_specs=pl.BlockSpec(memory_space=pltpu.VMEM),
        scratch_shapes=[
            vm((row_count, width), bf),
            vm((chips, width, 2 * cols), bf),
            vm((replicas, rank, width), bf),
            vm((replicas, rank, cols), bf),
            vm((chips, row_count, cols), f32),
            vm((chips, row_count, cols), bf),
            vm((chips, row_count, cols), bf),
            vm((chips, row_count, cols), bf),
            vm((chips, row_count, cols), bf),
            vm((row_count, 2 * rank), f32),
            vm((2, quarter, 2 * rank), bf),
            vm((2, quarter, 2 * rank), bf),
            vm((2, quarter, 2 * rank), bf),
            vm((chips, 2, quarter, 2 * rank), bf),
            vm((row_count, TOGETHER * rank), jnp.int32),
            vm((row_count, HEAD), f32),
            vm((row_count, HEAD), f32),
            vm((requests, HEAD), f32),
            dma((chunks,)), dma((chips, 2)), dma((2,)),
            dma((replicas, pieces, 2)), dma((replicas, pieces)),
            dma((replicas, groups, pieces)), dma((replicas, groups, pieces)),
            dma((replicas,)), dma((replicas,)),
            dma((chips, chunks)), dma((chips, chunks)),
            dma((chips, chunks)), dma((chips, chunks)),
            dma, dma,
            dma((chips, 2)), dma((chips, 2)),
        ],
        compiler_params=pltpu.CompilerParams(
            collective_id=0, has_side_effects=True, vmem_limit_bytes=60 * 1024 * 1024
        ),
        cost_estimate=pl.CostEstimate(
            flops=2 * row_count * width * (2 * chips * cols + replicas * rank),
            bytes_accessed=2 * width * (row_count + 2 * chips * cols),
            transcendentals=0,
        ),
    )(rows, adapters.reshape(requests), spans, keys, down[0].T, up[0])


def solution(mesh):
    in_specs = (
        P(("groups", "replica"), "tensor"),
        P(("groups", "replica"), None),
        P(("groups", "replica")),
        P("tensor", None),
        P("replica", "tensor", None),
        P("replica", None, "tensor"),
    )
    out_specs = P(("groups", "replica"), "tensor")
    sizes = (mesh.shape["groups"], mesh.shape["replica"], mesh.shape["tensor"] // 2, 3)
    sizes += (max(1, 16 // sizes[1]),)
    return jax.shard_map(
        functools.partial(on_device, sizes), mesh=mesh, in_specs=in_specs, out_specs=out_specs, check_vma=False
    )
```

time: 39.1 us -> 30.3 us (0.77)
  Pallas kernels: 33.1 us -> 28.3 us
  local copies, waits for them, and re-layouts: 5.65 us -> 1.77 us
    pallas_call x1, Pallas kernels: 33.1 us -> 28.3 us  [on_device(): pl.pallas_call(functools.partial(kernel, sizes), out_shape=jax.ShapeDtype...]
    unnamed x11 -> x1, local copies, waits for them, and re-layouts: 5.65 us -> 1.77 us
where the time goes in v2:
time: 30.3 us; the launch traced here: 30.1 us
  Pallas kernels  28.3 us (93%)
  local copies, waits for them, and re-layouts  1.77 us (6%)
    pallas_call x1, Pallas kernels, on_device(): pl.pallas_call(functools.partial(kernel, sizes), out_shape=jax.ShapeDtype...  28.3 us
    unnamed x1, local copies, waits for them, and re-layouts  1.77 us

profile of v2, /device:TPU:1, one launch (start us, length us, event | category | flops | bytes accessed | tf_op | source)
XLA Modules:
  0.0 30.1 jit_solution(15927205451656487155)
XLA Ops:
  0.0 28.3 %shard_map.64 = bf16[768,256]{1,0:T(8,128)(2,1)} custom-call(bf16[768,2048]{1,0:T(8,128)(2,1)} %x_hbm.1, s32[24]{0:T(128)} %bitcast.7, s32[24]{0:T(128)} %span_ref.1, bf16[2048,1024]{1,0:T(8,128)(2,1)} %k_hbm.1, bf16[64,2048]{1,0:T(8,128)(2,1)} %bitcast.5, bf16[64,256]{1,0:T(8,128)(2,1)} %bitcast.6), custom_call_target="tpu_custom_call" | custom-call | flops 4026531840 | bytes 7340032 | tf_op jit(solution)/shard_map/pallas_call | solution.py:345
  28.4 1.8 %copy.8 = bf16[768,256]{1,0:T(8,128)(2,1)} copy(bf16[768,256]{1,0:T(8,128)(2,1)} %shard_map.64) | data formatting | bytes 786432

commit v3 on v2

--- a/solution.py
+++ b/solution.py
@@ -261,35 +261,44 @@
     packed = jnp.where(low, zacc[:mid, :], zacc[mid:, :])
     for h in range(2):
         zsend[h] = packed[h * quarter : (h + 1) * quarter].astype(jnp.bfloat16)
-    z_copy = pltpu.make_async_remote_copy(
-        src_ref=zsend, dst_ref=zrecv, send_sem=z_ssem, recv_sem=z_rsem,
-        device_id={"tensor": partner}, device_id_type=MESH,
-    )
-    z_copy.start()
-    z_copy.wait()
+    def z_copy(i):
+        given, taken = ((1 - core, core), (core, 1 - core))[i]
+        return [
+            pltpu.make_async_remote_copy(
+                src_ref=zsend.at[h], dst_ref=zrecv.at[h], send_sem=z_ssem.at[i], recv_sem=z_rsem.at[i],
+                device_id={"tensor": partner}, device_id_type=MESH,
+            )
+            for h in (given, taken)
+        ]
+
+    for i in range(2):
+        z_copy(i)[0].start()
+    z_copy(0)[1].wait_recv()
+    zchip[core] = (zsend[core].astype(jnp.float32) + zrecv[core].astype(jnp.float32)).astype(jnp.bfloat16)
+
+    def z_over(d, c):
+        return pltpu.make_async_remote_copy(
+            src_ref=zchip.at[core], dst_ref=zx.at[d, core],
+            send_sem=zx_ssem.at[d, c], recv_sem=zx_rsem.at[d, core],
+            device_id={"tensor": chip_at(d) * 2 + c}, device_id_type=MESH,
+        )
+
+    def z_arrival(d, c):
+        return pltpu.make_async_remote_copy(
+            src_ref=zchip.at[c], dst_ref=zx.at[d, c],
+            send_sem=zx_ssem.at[d, c], recv_sem=zx_rsem.at[d, c],
+            device_id={"tensor": chip_at(d) * 2 + c}, device_id_type=MESH,
+        )
+
+    for d in range(1, chips):
+        for c in range(2):
+            z_over(d, c).start()
+    z_copy(1)[1].wait_recv()
+    for i in range(2):
+        z_copy(i)[0].wait_send()
     chip_sum = [
         packed[h * quarter : (h + 1) * quarter] + zrecv[h].astype(jnp.float32) for h in range(2)
     ]
-    for h in range(2):
-        zchip[h] = chip_sum[h].astype(jnp.bfloat16)
-
-    def z_over(d, c):
-        return pltpu.make_async_remote_copy(
-            src_ref=zchip.at[core], dst_ref=zx.at[d, core],
-            send_sem=zx_ssem.at[d, c], recv_sem=zx_rsem.at[d, core],
-            device_id={"tensor": chip_at(d) * 2 + c}, device_id_type=MESH,
-        )
-
-    def z_arrival(d, c):
-        return pltpu.make_async_remote_copy(
-            src_ref=zchip.at[c], dst_ref=zx.at[d, c],
-            send_sem=zx_ssem.at[d, c], recv_sem=zx_rsem.at[d, c],
-            device_id={"tensor": chip_at(d) * 2 + c}, device_id_type=MESH,
-        )
-
-    for d in range(1, chips):
-        for c in range(2):
-            z_over(d, c).start()
     loads["up"].wait()
     for j in range(1, replicas):
         up_arrival(j).wait()
@@ -372,7 +381,7 @@
             dma((replicas,)), dma((replicas,)),
             dma((chips, chunks)), dma((chips, chunks)),
             dma((chips, chunks)), dma((chips, chunks)),
-            dma, dma,
+            dma((2,)), dma((2,)),
             dma((chips, 2)), dma((chips, 2)),
         ],
         compiler_params=pltpu.CompilerParams(

time: 30.3 us -> 30.2 us (level)
  no operation moved by 1% of the time
where the time goes in v3:
time: 30.2 us; the launch traced here: 30 us
  Pallas kernels  28.2 us (93%)
  local copies, waits for them, and re-layouts  1.77 us (6%)
    pallas_call x1, Pallas kernels, on_device(): pl.pallas_call(functools.partial(kernel, sizes), out_shape=jax.ShapeDtype...  28.2 us
    unnamed x1, local copies, waits for them, and re-layouts  1.77 us

profile of v3, /device:TPU:1, one launch (start us, length us, event | category | flops | bytes accessed | tf_op | source)
XLA Modules:
  0.0 30.0 jit_solution(14901077657403856562)
XLA Ops:
  0.0 28.2 %shard_map.64 = bf16[768,256]{1,0:T(8,128)(2,1)} custom-call(bf16[768,2048]{1,0:T(8,128)(2,1)} %x_hbm.1, s32[24]{0:T(128)} %bitcast.7, s32[24]{0:T(128)} %span_ref.1, bf16[2048,1024]{1,0:T(8,128)(2,1)} %k_hbm.1, bf16[64,2048]{1,0:T(8,128)(2,1)} %bitcast.5, bf16[64,256]{1,0:T(8,128)(2,1)} %bitcast.6), custom_call_target="tpu_custom_call" | custom-call | flops 4026531840 | bytes 7340032 | tf_op jit(solution)/shard_map/pallas_call | solution.py:354
  28.2 1.8 %copy.8 = bf16[768,256]{1,0:T(8,128)(2,1)} copy(bf16[768,256]{1,0:T(8,128)(2,1)} %shard_map.64) | data formatting | bytes 786432
